TPU v7x, 32 devices: a whole 2x2x4 slice. The times are simulated.
32 devices in a mesh: bx: 16 (over z, y, x), by: 2 (over core).
Axes of the slice: x: 2, y: 2, z: 4, core: 2. Of those that a mesh axis runs over, the one named last changes fastest.
Arguments:
- density: float32 [4, 128, 256], P(None, 'bx', 'by'), may hold values from 0.7 to 1.4
- velocity: float32 [3, 4, 128, 256], P(None, None, 'bx', 'by'), may hold values from -4 to 4
- pressure: float32 [4, 128, 256], P(None, 'bx', 'by'), may hold values from 0.7 to 1.4
- field: float32 [3, 4, 128, 256], P(None, None, 'bx', 'by'), may hold values from -4 to 4
Outputs:
- new_density: float32 [4, 128, 256], P(None, 'bx', 'by')
- new_momentum: float32 [3, 4, 128, 256], P(None, None, 'bx', 'by')
- new_energy: float32 [4, 128, 256], P(None, 'bx', 'by')
- new_field: float32 [3, 4, 128, 256], P(None, None, 'bx', 'by')
- time_step: float32 [], replicated
All inputs are finite; a program needn't handle non-finite values.
Results may differ from a plain program's by a relative error of at most 0.0003.
Values sent between devices are 32-bit elements; how exact they have to be, the bound alone decides.
A program may use at most 64 MiB of HBM per device.

v0:
```python
import jax
import jax.numpy as jnp
from jax import lax
from jax.sharding import PartitionSpec as P

GAMMA = 5.0 / 3.0
CFL = 0.3
AXES = (1, 2, 0)
first_rim = 3
second_rim = 4


def with_halo(cells, sides, width):
    for axis, dim in sides:
        count = lax.axis_size(axis)
        head = lax.slice_in_dim(cells, 0, width, axis=dim)
        tail = lax.slice_in_dim(cells, cells.shape[dim] - width, cells.shape[dim], axis=dim)
        cells = jnp.concatenate(
            [
                lax.ppermute(tail, axis, [(i, (i + 1) % count) for i in range(count)]),
                cells,
                lax.ppermute(head, axis, [((i + 1) % count, i) for i in range(count)]),
            ],
            axis=dim,
        )
    return cells


def moved(array, by, comp):
    return jnp.roll(array, by, AXES[comp])


def fast_speed(rho, pres, normal, trans_one, trans_two):
    sound = GAMMA * pres / rho
    along = normal * normal / rho
    across = (trans_one * trans_one + trans_two * trans_two) / rho
    inner = (sound - along) ** 2 + across * (across + 2.0 * sound + 2.0 * along)
    return jnp.sqrt(0.5 * (sound + along + across + jnp.sqrt(inner)))


def centered(face):
    return [0.5 * (face[c] + moved(face[c], -1, c)) for c in range(3)]


def unpack(stack):
    return (stack[0], [stack[1], stack[2], stack[3]], stack[4], [stack[5], stack[6], stack[7]])


def speeds(stack):
    rho, vel, pres, face = unpack(stack)
    cell = centered(face)
    best = None
    for c in range(3):
        value = jnp.abs(vel[c]) + fast_speed(
            rho, pres, cell[c], cell[(c + 1) % 3], cell[(c + 2) % 3]
        )
        best = value if best is None else jnp.maximum(best, value)
    return best


def conserved(rho, vel, pres, cell):
    bsq = cell[0] * cell[0] + cell[1] * cell[1] + cell[2] * cell[2]
    vsq = vel[0] * vel[0] + vel[1] * vel[1] + vel[2] * vel[2]
    energy = pres / (GAMMA - 1.0) + 0.5 * rho * vsq + 0.5 * bsq
    return [rho, rho * vel[0], rho * vel[1], rho * vel[2], energy]


def side_terms(prim, normal, comp):
    rho, vel, pres = (prim[0], prim[1:4], prim[4])
    mag = list(prim[5:8])
    mag[comp] = normal
    one, two = ((comp + 1) % 3, (comp + 2) % 3)
    bsq = mag[0] * mag[0] + mag[1] * mag[1] + mag[2] * mag[2]
    total = pres + 0.5 * bsq
    cons = conserved(rho, vel, pres, mag)
    vnorm = vel[comp]
    vdotb = vel[0] * mag[0] + vel[1] * mag[1] + vel[2] * mag[2]
    flux = [rho * vnorm]
    for k in range(3):
        term = rho * vel[k] * vnorm - mag[k] * normal
        flux.append(term + total if k == comp else term)
    flux.append((cons[4] + total) * vnorm - normal * vdotb)
    flux.append(mag[one] * vnorm - normal * vel[one])
    flux.append(mag[two] * vnorm - normal * vel[two])
    cons = cons + [mag[one], mag[two]]
    return (cons, flux, vnorm, fast_speed(rho, pres, normal, mag[one], mag[two]))


def hlle(left, right, normal, comp):
    cons_left, flux_left, vel_left, fast_left = side_terms(left, normal, comp)
    cons_right, flux_right, vel_right, fast_right = side_terms(right, normal, comp)
    lower = jnp.minimum(jnp.minimum(vel_left - fast_left, vel_right - fast_right), 0.0)
    upper = jnp.maximum(jnp.maximum(vel_left + fast_left, vel_right + fast_right), 0.0)
    spread = upper - lower
    return [
        (
            upper * flux_left[v]
            - lower * flux_right[v]
            + lower * upper * (cons_right[v] - cons_left[v])
        )
        / spread
        for v in range(7)
    ]


def minmod(first, second):
    return jnp.where(
        first * second > 0.0, jnp.sign(first) * jnp.minimum(jnp.abs(first), jnp.abs(second)), 0.0
    )


def fluxes(stack, slopes):
    rho, vel, pres, face = unpack(stack)
    cell = centered(face)
    prim = [rho, vel[0], vel[1], vel[2], pres, cell[0], cell[1], cell[2]]
    result = []
    for c in range(3):
        if slopes:
            grads = [minmod(q - moved(q, 1, c), moved(q, -1, c) - q) for q in prim]
            left = [moved(q + 0.5 * g, 1, c) for q, g in zip(prim, grads)]
            right = [q - 0.5 * g for q, g in zip(prim, grads)]
        else:
            left = [moved(q, 1, c) for q in prim]
            right = prim
        result.append(hlle(left, right, face[c], c))
    return result


def changes(flux):
    div = []
    for v in range(5):
        total = None
        for c in range(3):
            term = moved(flux[c][v], -1, c) - flux[c][v]
            total = term if total is None else total + term
        div.append(total)
    fx, fy, fz = flux
    ez = 0.25 * (-fx[5] - moved(fx[5], 1, 1) + fy[6] + moved(fy[6], 1, 0))
    ex = 0.25 * (-fy[5] - moved(fy[5], 1, 2) + fz[6] + moved(fz[6], 1, 1))
    ey = 0.25 * (-fz[5] - moved(fz[5], 1, 0) + fx[6] + moved(fx[6], 1, 2))
    curl = [
        moved(ez, -1, 1) - ez - (moved(ey, -1, 2) - ey),
        moved(ex, -1, 2) - ex - (moved(ez, -1, 0) - ez),
        moved(ey, -1, 0) - ey - (moved(ex, -1, 1) - ex),
    ]
    return (div, curl)


def base(stack):
    rho, vel, pres, face = unpack(stack)
    start = conserved(rho, vel, pres, centered(face))
    return jnp.stack(start + face)


def half_state(stack, step):
    rho, vel, pres, face = unpack(stack)
    start = conserved(rho, vel, pres, centered(face))
    div, curl = changes(fluxes(stack, False))
    cons = [start[v] - 0.5 * step * div[v] for v in range(5)]
    newface = [face[c] - 0.5 * step * curl[c] for c in range(3)]
    cell = centered(newface)
    hrho = cons[0]
    hvel = [cons[k + 1] / hrho for k in range(3)]
    msq = cons[1] * cons[1] + cons[2] * cons[2] + cons[3] * cons[3]
    bsq = cell[0] * cell[0] + cell[1] * cell[1] + cell[2] * cell[2]
    hpres = (GAMMA - 1.0) * (cons[4] - 0.5 * msq / hrho - 0.5 * bsq)
    return jnp.stack([hrho] + hvel + [hpres] + newface)


def correction(half):
    div, curl = changes(fluxes(half, True))
    return jnp.stack(div + curl)


def trimmed(array, width):
    return array[..., width:-width, width:-width]


def on_device(density, velocity, pressure, field):
    stack = jnp.concatenate([density[None], velocity, pressure[None], field], axis=0)
    wide = with_halo(stack, (("bx", 2), ("by", 3)), first_rim)
    top = lax.pmax(jnp.max(trimmed(speeds(wide), first_rim)), ("bx", "by"))
    step = CFL / top
    half = trimmed(half_state(wide, step), first_rim)
    beside_all = with_halo(half, (("bx", 2), ("by", 3)), second_rim)
    final = trimmed(base(wide), first_rim) - step * trimmed(correction(beside_all), second_rim)
    return (final[0], final[1:4], final[4], final[5:8], step)


def solution(mesh):
    in_specs = (
        P(None, "bx", "by"),
        P(None, None, "bx", "by"),
        P(None, "bx", "by"),
        P(None, None, "bx", "by"),
    )
    out_specs = (
        P(None, "bx", "by"),
        P(None, None, "bx", "by"),
        P(None, "bx", "by"),
        P(None, None, "bx", "by"),
        P(),
    )
    return jax.shard_map(
        on_device, mesh=mesh, in_specs=in_specs, out_specs=out_specs, check_vma=False
    )
```

profile of v0, /device:TPU:0, one launch (start us, length us, event | category | flops | bytes accessed | tf_op | source)
XLA Modules:
  0.0 131.1 jit_solution(2164584577307522797)
XLA Ops:
  0.6 0.9 pad_maximum_fusion.4
  1.6 3.0 %collective-permute-start = (f32[8,4,3,128]{3,2,1,0:T(4,128)S(1)}, f32[8,4,3,128]{3,2,1,0:T(4,128)S(1)}, u32[]{:S(2)}, u32[]{:S(2)}) collective-permute-start(f32[8,4,3,128]{3,2,1,0:T(4,128)S(1)} %get-tuple-element.248), channel_id=1, source_target_pairs={{0,2},{2,4},{4,6},{6,8},{8,10},{10,12},{12,14},{14,16},{16,18},{18... | collective-permute-start | bytes 147464 | tf_op jit(solution)/shard_map/ppermute | solution.py:20
  4.6 4.1 %collective-permute-start.1 = (f32[8,4,3,128]{3,2,1,0:T(4,128)S(1)}, f32[8,4,3,128]{3,2,1,0:T(4,128)S(1)}, u32[]{:S(2)}, u32[]{:S(2)}) collective-permute-start(f32[8,4,3,128]{3,2,1,0:T(4,128)S(1)} %get-tuple-element.249), channel_id=1, source_target_pairs={{2,0},{4,2},{6,4},{8,6},{10,8},{12,10},{14,12},{16,14},{18,16},{20... | collective-permute-start | bytes 147464 | tf_op jit(solution)/shard_map/ppermute | solution.py:22
  8.6 2.2 %collective-permute-done = f32[8,4,3,128]{3,2,1,0:T(4,128)S(1)} collective-permute-done((f32[8,4,3,128]{3,2,1,0:T(4,128)S(1)}, f32[8,4,3,128]{3,2,1,0:T(4,128)S(1)}, u32[]{:S(2)}, u32[]{:S(2)}) %collective-permute-start) | collective-permute-done | bytes 49184 | tf_op jit(solution)/shard_map/ppermute | solution.py:20
  11.7 1.0 collective-permute-done.2
  13.5 0.6 fusion.378
  16.0 0.7 fusion.384
  16.7 0.7 slice_bitcast_fusion.181
  18.6 0.7 slice_bitcast_fusion.183
  20.0 0.6 slice_bitcast_fusion.289
  20.7 0.6 slice_bitcast_fusion.291
  22.7 0.7 slice_bitcast_fusion.24
  24.2 0.7 slice_bitcast_fusion.16
  26.3 0.6 slice_bitcast_fusion.216
  29.5 0.6 slice_bitcast_fusion.17
  31.6 0.6 slice_bitcast_fusion.25
  32.9 0.6 slice_bitcast_fusion.218
  33.5 0.7 slice_bitcast_fusion.174
  34.2 0.6 slice_bitcast_fusion.282
  37.2 0.6 slice_bitcast_fusion.39
  39.2 0.6 slice_bitcast_fusion.43
  40.5 0.6 slice_bitcast_fusion.279
  42.3 0.6 slice_bitcast_fusion.217
  43.0 0.6 slice_bitcast_fusion.276
  44.3 0.6 slice_bitcast_fusion.281
  46.2 0.6 slice_bitcast_fusion.277
  46.9 0.7 slice_bitcast_fusion.280
  47.6 0.7 slice_bitcast_fusion.170
  48.3 0.6 slice_bitcast_fusion.278
  49.6 0.6 slice_bitcast_fusion.215
  50.2 0.7 slice_bitcast_fusion.275
  50.9 0.7 fusion.329
  51.6 0.6 slice_bitcast_fusion.107
  52.3 40.4 %pmax.7 = f32[]{:T(128)} all-reduce(f32[]{:T(128)} %fusion.329), channel_id=1, replica_groups=mesh['bx'=16,'by'=2] {'bx','by'}, use_global_device_ids=true, to_apply=%region_1.2 | all-reduce | flops 1 | bytes 8 | tf_op jit(solution)/shard_map/pmax | solution.py:182
  93.4 0.7 copy-done.39
  94.1 1.1 fusion.73
  96.4 0.7 constant_dynamic-update-slice_fusion.8
  97.2 0.7 copy-done.17
  101.4 1.4 %fusion.30 = (f32[8,4,14,134]{3,2,1,0:T(8,128)S(1)}, f32[1,4,14,134]{3,2,1,0:T(8,128)S(1)}, f32[1,4,14,134]{3,2,1,0:T(8,128)S(1)}, f32[1,4,14,134]{3,2,1,0:T(8,128)S(1)}) fusion(f32[8,4,14,134]{3,2,1,0:T(8,128)S(1)} %divide_dynamic-update-slice_fusion, f32[1,4,1,134]{3,2,1,0:T(1,128)S(1)} %copy-done.54, f32[1,4,13,134]{3,2,1,0:T(8,128)S(1)} %copy-done.7, ...), kind=kLoop, calls=%fused_computation.124 | loop fusion | flops 3849552 | bytes 5308420
  103.1 2.3 %collective-permute-start.4 = (f32[8,4,4,128]{3,2,1,0:T(4,128)S(1)}, f32[8,4,4,128]{3,2,1,0:T(4,128)S(1)}, u32[]{:S(2)}, u32[]{:S(2)}) collective-permute-start(f32[8,4,4,128]{3,2,1,0:T(4,128)S(1)} %get-tuple-element.197), channel_id=1, source_target_pairs={{0,2},{2,4},{4,6},{6,8},{8,10},{10,12},{12,14},{14,16},{16,18},{18... | collective-permute-start | bytes 196616 | tf_op jit(solution)/shard_map/ppermute | solution.py:20
  105.5 3.3 %collective-permute-start.5 = (f32[8,4,4,128]{3,2,1,0:T(4,128)S(1)}, f32[8,4,4,128]{3,2,1,0:T(4,128)S(1)}, u32[]{:S(2)}, u32[]{:S(2)}) collective-permute-start(f32[8,4,4,128]{3,2,1,0:T(4,128)S(1)} %get-tuple-element.198), channel_id=1, source_target_pairs={{2,0},{4,2},{6,4},{8,6},{10,8},{12,10},{14,12},{16,14},{18,16},{20... | collective-permute-start | bytes 196616 | tf_op jit(solution)/shard_map/ppermute | solution.py:22
  108.9 2.1 %collective-permute-done.4 = f32[8,4,4,128]{3,2,1,0:T(4,128)S(1)} collective-permute-done((f32[8,4,4,128]{3,2,1,0:T(4,128)S(1)}, f32[8,4,4,128]{3,2,1,0:T(4,128)S(1)}, u32[]{:S(2)}, u32[]{:S(2)}) %collective-permute-start.4) | collective-permute-done | bytes 65568 | tf_op jit(solution)/shard_map/ppermute | solution.py:20
  112.2 0.7 collective-permute-done.6
  117.6 0.6 add_divide_fusion.1
  119.8 0.6 add_divide_fusion
  123.8 1.6 %fusion.80 = (f32[8,4,16,136]{3,2,1,0:T(8,128)S(1)}, f32[1,4,16,136]{3,2,1,0:T(8,128)S(1)}, f32[1,4,16,136]{3,2,1,0:T(8,128)S(1)}, f32[1,4,16,136]{3,2,1,0:T(8,1...) fusion(f32[1,4,1,136]{3,2,1,0:T(1,128)S(1)} %slice_bitcast_fusi, ...), kind=kLoop, calls=%fused_computation.215 | loop fusion | flops 3620863 | bytes 3627008
  126.9 0.8 fusion.96
  129.3 0.6 fusion.382
  (400 shorter events, 39.5 us)
Async XLA Ops:
  1.5 9.4 %copy-start = (f32[3,4,8,128]{3,2,1,0:T(8,128)S(1)}, f32[3,4,8,128]{3,2,1,0:T(8,128)}, u32[]{:S(2)}) copy-start(f32[3,4,8,128]{3,2,1,0:T(8,128)} %param.7) | copy-start | bytes 147460
  1.5 9.4 %copy-start.1 = (f32[3,4,8,128]{3,2,1,0:T(8,128)S(1)}, f32[3,4,8,128]{3,2,1,0:T(8,128)}, u32[]{:S(2)}) copy-start(f32[3,4,8,128]{3,2,1,0:T(8,128)} %param.5) | copy-start | bytes 147460
  1.5 9.4 %copy-start.21 = (f32[4,8,128]{2,1,0:T(8,128)S(1)}, f32[4,8,128]{2,1,0:T(8,128)}, u32[]{:S(2)}) copy-start(f32[4,8,128]{2,1,0:T(8,128)} %param.6) | copy-start | bytes 49156
  1.5 9.4 %copy-start.22 = (f32[4,8,128]{2,1,0:T(8,128)S(1)}, f32[4,8,128]{2,1,0:T(8,128)}, u32[]{:S(2)}) copy-start(f32[4,8,128]{2,1,0:T(8,128)} %param.4) | copy-start | bytes 49156
  1.6 9.3 %collective-permute-start = (f32[8,4,3,128]{3,2,1,0:T(4,128)S(1)}, f32[8,4,3,128]{3,2,1,0:T(4,128)S(1)}, u32[]{:S(2)}, u32[]{:S(2)}) collective-permute-start(f32[8,4,3,128]{3,2,1,0:T(4,128)S(1)} %get-tuple-element.248), channel_id=1, source_target_pairs={{0,2},{2,4},{4,6},{6,8},{8,10},{10,12},{12,14},{14,16},{16,18},{18... | collective-permute-start | bytes 147464 | tf_op jit(solution)/shard_map/ppermute | solution.py:20
  4.6 6.3 %collective-permute-start.1 = (f32[8,4,3,128]{3,2,1,0:T(4,128)S(1)}, f32[8,4,3,128]{3,2,1,0:T(4,128)S(1)}, u32[]{:S(2)}, u32[]{:S(2)}) collective-permute-start(f32[8,4,3,128]{3,2,1,0:T(4,128)S(1)} %get-tuple-element.249), channel_id=1, source_target_pairs={{2,0},{4,2},{6,4},{8,6},{10,8},{12,10},{14,12},{16,14},{18,16},{20... | collective-permute-start | bytes 147464 | tf_op jit(solution)/shard_map/ppermute | solution.py:22
  11.1 1.6 %collective-permute-start.2 = (f32[8,4,14,3]{3,2,1,0:T(8,128)S(1)}, f32[8,4,14,3]{3,2,1,0:T(8,128)S(1)}, u32[]{:S(2)}, u32[]{:S(2)}) collective-permute-start(f32[8,4,14,3]{3,2,1,0:T(8,128)S(1)} %get-tuple-element.242), channel_id=1, source_target_pairs={{0,1},{1,0},{2,3},{3,2},{4,5},{5,4},{6,7},{7,6},{8,9},{9,8},{10,11... | collective-permute-start | bytes 16136 | tf_op jit(solution)/shard_map/ppermute | solution.py:20
  11.2 1.9 %collective-permute-start.3 = (f32[8,4,14,3]{3,2,1,0:T(8,128)S(1)}, f32[8,4,14,3]{3,2,1,0:T(8,128)S(1)}, u32[]{:S(2)}, u32[]{:S(2)}) collective-permute-start(f32[8,4,14,3]{3,2,1,0:T(8,128)S(1)} %get-tuple-element.243), channel_id=1, source_target_pairs={{1,0},{0,1},{3,2},{2,3},{5,4},{4,5},{7,6},{6,7},{9,8},{8,9},{11,10... | collective-permute-start | bytes 16136 | tf_op jit(solution)/shard_map/ppermute | solution.py:22
  16.0 1.3 %copy-start.35 = (f32[8,4,14,134]{3,2,1,0:T(8,128)}, f32[8,4,14,134]{3,2,1,0:T(8,128)S(1)}, u32[]{:S(2)}) copy-start(f32[8,4,14,134]{3,2,1,0:T(8,128)S(1)} %get-tuple-element.5) | copy-start | bytes 720388
  95.3 0.8 copy-start.15
  95.3 0.8 copy-start.26
  95.3 0.8 copy-start.27
  95.3 0.8 copy-start.33
  95.3 0.8 copy-start.34
  95.4 0.8 copy-start.42
  95.4 0.9 copy-start.11
  95.4 0.9 copy-start.9
  95.4 0.9 copy-start.10
  95.5 0.9 copy-start.8
  95.5 0.9 copy-start.25
  96.4 0.8 copy-start.20
  100.0 0.8 copy-start.2
  100.0 0.9 copy-start.3
  100.0 0.9 copy-start.4
  100.0 0.9 copy-start.5
  100.0 1.0 copy-start.6
  100.0 1.0 copy-start.7
  100.0 1.0 copy-start.12
  100.0 1.0 copy-start.13
  100.0 1.0 copy-start.14
  100.0 1.0 copy-start.29
  100.0 1.0 copy-start.30
  100.1 1.0 copy-start.31
  100.1 1.0 copy-start.37
  100.1 0.9 copy-start.38
  100.1 0.9 copy-start.40
  100.1 0.9 copy-start.45
  100.1 0.9 copy-start.46
  100.1 0.9 copy-start.52
  100.1 0.9 copy-start.53
  100.1 0.9 copy-start.54
  100.5 0.8 copy-start.23
  100.6 0.8 copy-start.24
  103.1 7.9 %collective-permute-start.4 = (f32[8,4,4,128]{3,2,1,0:T(4,128)S(1)}, f32[8,4,4,128]{3,2,1,0:T(4,128)S(1)}, u32[]{:S(2)}, u32[]{:S(2)}) collective-permute-start(f32[8,4,4,128]{3,2,1,0:T(4,128)S(1)} %get-tuple-element.197), channel_id=1, source_target_pairs={{0,2},{2,4},{4,6},{6,8},{8,10},{10,12},{12,14},{14,16},{16,18},{18... | collective-permute-start | bytes 196616 | tf_op jit(solution)/shard_map/ppermute | solution.py:20
  105.5 5.6 %collective-permute-start.5 = (f32[8,4,4,128]{3,2,1,0:T(4,128)S(1)}, f32[8,4,4,128]{3,2,1,0:T(4,128)S(1)}, u32[]{:S(2)}, u32[]{:S(2)}) collective-permute-start(f32[8,4,4,128]{3,2,1,0:T(4,128)S(1)} %get-tuple-element.198), channel_id=1, source_target_pairs={{2,0},{4,2},{6,4},{8,6},{10,8},{12,10},{14,12},{16,14},{18,16},{20... | collective-permute-start | bytes 196616 | tf_op jit(solution)/shard_map/ppermute | solution.py:22
  111.1 1.0 copy-start.36
  111.3 1.6 %collective-permute-start.6 = (f32[8,4,16,4]{3,2,1,0:T(8,128)S(1)}, f32[8,4,16,4]{3,2,1,0:T(8,128)S(1)}, u32[]{:S(2)}, u32[]{:S(2)}) collective-permute-start(f32[8,4,16,4]{3,2,1,0:T(8,128)S(1)} %get-tuple-element.240), channel_id=1, source_target_pairs={{0,1},{1,0},{2,3},{3,2},{4,5},{5,4},{6,7},{7,6},{8,9},{9,8},{10,11... | collective-permute-start | bytes 24584 | tf_op jit(solution)/shard_map/ppermute | solution.py:20
  111.3 1.9 %collective-permute-start.7 = (f32[8,4,16,4]{3,2,1,0:T(8,128)S(1)}, f32[8,4,16,4]{3,2,1,0:T(8,128)S(1)}, u32[]{:S(2)}, u32[]{:S(2)}) collective-permute-start(f32[8,4,16,4]{3,2,1,0:T(8,128)S(1)} %get-tuple-element.241), channel_id=1, source_target_pairs={{1,0},{0,1},{3,2},{2,3},{5,4},{4,5},{7,6},{6,7},{9,8},{8,9},{11,10... | collective-permute-start | bytes 24584 | tf_op jit(solution)/shard_map/ppermute | solution.py:22
  (15 other events, 10.9 us)
where the time goes:
time: 132 us; the launch traced here: 131 us
  local copies, waits for them, and re-layouts  44.6 us (34%)
  blocking collectives  40.4 us (31%)
  other arithmetic  21 us (16%)
  starting transfers between devices  13.9 us (11%)
  waiting for transfers between devices  6.84 us (5%)
  between operations  4.36 us (3%)
    pmax x1, blocking collectives, on_device(): top = lax.pmax(jnp.max(trimmed(speeds(wide), first_rim)), ('bx', 'by'))  40.4 us
    concatenate x220, local copies, waits for them, and re-layouts, moved(): return jnp.roll(array, by, AXES[comp])  36 us
    ppermute x4, starting transfers between devices, with_halo(): lax.ppermute(head, axis, [((i + 1) % count, i) for i in range(count)])  8.4 us
    unnamed x17, other arithmetic  8.21 us
    div x34, other arithmetic, hlle(): (upper * flux_left[v] - lower * flux_right[v] + lower * upper * (cons_rig...  6.55 us
    ppermute x4, waiting for transfers between devices, with_halo(): lax.ppermute(tail, axis, [(i, (i + 1) % count) for i in range(count)])  6.08 us
    ppermute x4, starting transfers between devices, with_halo(): lax.ppermute(tail, axis, [(i, (i + 1) % count) for i in range(count)])  5.46 us
    unnamed x111, local copies, waits for them, and re-layouts  4.78 us
  transfers between devices with their start and end apart: 8, of which 6 were waited for; matrix products, arithmetic and copies ran while one was open for 0% of the time, Pallas kernels for 0%

commit v1 on v0

v1 whole, which is shorter than its diff:
```python
import functools

import jax
import jax.numpy as jnp
from jax import lax
from jax.experimental import pallas as pl
from jax.experimental.pallas import tpu as pltpu
from jax.sharding import PartitionSpec as P

GAMMA = 5.0 / 3.0
CFL = 0.3
TINY = 1e-30
CZ, CX, CY = 4, 8, 128
EDGE = 4
CHUNKS = 5
HALOS = ((1, 0), (-1, 0), (0, 1), (0, -1), (1, 1), (1, -1), (-1, 1), (-1, -1))


def max_stages(nbx, nby):
    stages = [[(0, o) for o in range(1, nby)]]
    window = 1
    while window < nbx:
        stages.append([(m * window, 0) for m in (1, 2, 3) if m * window < nbx])
        window *= 4
    return [s for s in stages if s]


def roll(a, by, axis):
    by = by % a.shape[axis]
    return a if by == 0 else pltpu.roll(a, by, axis)


def lanes():
    return lax.broadcasted_iota(jnp.int32, (1, CY), 1)


def shifted(ref, v, k, by, c):
    if c == 0:
        return roll(ref[v, k], by, 0)
    if c == 2:
        return ref[v, (k - by) % CZ] if k < EDGE else roll(ref[v, k], 32 * by, 1)
    body = roll(ref[v, k], by, 1)
    if k == EDGE:
        return body
    if by == 1:
        return jnp.where(lanes() == 0, roll(ref[v, EDGE], -(32 * k + 7), 1), body)
    return jnp.where(lanes() == CY - 1, roll(ref[v, EDGE], CY - 1 - (32 * k + 24), 1), body)


def root(y):
    return y * lax.rsqrt(jnp.maximum(y, TINY))


def fast(rho, pres, n, t):
    a = GAMMA * pres
    s = a + n
    d = a - n
    x = 0.5 * (s + t + root(d * d + t * (t + 2.0 * s)))
    return x * lax.rsqrt(jnp.maximum(x * rho, TINY))


def part(side, bn, n, fastness, alpha_term, w):
    rho, vn, v1, v2, p, b1, b2, t = side
    half_bsq = 0.5 * (t + n)
    energy = 1.5 * p + (0.5 * rho) * (vn * vn + v1 * v1 + v2 * v2) + half_bsq
    wp = w * (p + half_bsq)
    beta = w * bn
    alpha = w * vn + alpha_term
    m = alpha * rho
    vb = vn * bn + v1 * b1 + v2 * b2
    return [
        m,
        m * vn - beta * bn + wp,
        m * v1 - beta * b1,
        m * v2 - beta * b2,
        alpha * energy + wp * vn - beta * vb,
        alpha * b1 - beta * v1,
        alpha * b2 - beta * v2,
    ]


def hlle(left, right, bn):
    n = bn * bn
    left = left + [left[5] * left[5] + left[6] * left[6]]
    right = right + [right[5] * right[5] + right[6] * right[6]]
    cl = fast(left[0], left[4], n, left[7])
    cr = fast(right[0], right[4], n, right[7])
    sl = jnp.minimum(jnp.minimum(left[1] - cl, right[1] - cr), 0.0)
    sr = jnp.maximum(jnp.maximum(left[1] + cl, right[1] + cr), 0.0)
    inv = 1.0 / (sr - sl)
    wl = sr * inv
    wr = -sl * inv
    wd = sl * wl
    fl = part(left, bn, n, cl, -wd, wl)
    fr = part(right, bn, n, cr, wd, wr)
    return [a + b for a, b in zip(fl, fr)]


def put_flux(flux, c, k, values):
    one, two = (c + 1) % 3, (c + 2) % 3
    for slot, value in zip((0, 1 + c, 1 + one, 1 + two, 4, 5, 6), values):
        flux[7 * c + slot, k] = value


def curl_parts(edge, c, k):
    one, two = (c + 1) % 3, (c + 2) % 3
    return (shifted(edge, two, k, -1, one) - edge[two, k]) - (
        shifted(edge, one, k, -1, two) - edge[one, k]
    )


def edges(flux, edge, ks):
    for k in ks:
        for e in range(3):
            a, b = (e + 1) % 3, (e + 2) % 3
            fa, fb = 7 * a + 5, 7 * b + 6
            edge[e, k] = 0.25 * (
                (flux[fb, k] + shifted(flux, fb, k, 1, a))
                - (flux[fa, k] + shifted(flux, fa, k, 1, b))
            )


def div_part(flux, v, k):
    total = None
    for c in range(3):
        term = shifted(flux, 7 * c + v, k, -1, c) - flux[7 * c + v, k]
        total = term if total is None else total + term
    return total


def strips(tiles):
    lane = lanes()
    merged = roll(tiles[0], 8, 1)
    for z in range(1, CZ):
        merged = jnp.where(lane >= 32 * z, roll(tiles[z], 8 + 32 * z, 1), merged)
    return jnp.where(lane % 32 < 16, merged, roll(merged, 16, 1))


def kernel(
    nbx, nby, stages,
    rho_in, vel_in, pres_in, face_in,
    rho_out, mom_out, ener_out, face_out, step_out,
    own, own_strip, halo, y_strip, d_strip, top_send, top_recv,
    state, cell, flux, edge, change, half, hcell, lefts, rights, result,
    in_sem, out_sem, send_sem, recv_sem, tsend_sem, trecv_sem,
):
    mx, my = lax.axis_index("bx"), lax.axis_index("by")

    def at(dx, dy):
        return (lax.rem(mx + dx % nbx, nbx), lax.rem(my + dy % nby, nby))

    loads = [
        pltpu.make_async_copy(rho_in, own.at[0], in_sem.at[0]),
        pltpu.make_async_copy(vel_in, own.at[pl.ds(1, 3)], in_sem.at[1]),
        pltpu.make_async_copy(pres_in, own.at[4], in_sem.at[2]),
        pltpu.make_async_copy(face_in, own.at[pl.ds(5, 3)], in_sem.at[3]),
    ]
    for copy in loads:
        copy.start()

    barrier = pltpu.get_barrier_semaphore()
    greeted = sorted(
        {(dx % nbx, dy % nby) for dx, dy in HALOS}
        | {((-dx) % nbx, (-dy) % nby) for stage in stages for dx, dy in stage}
    )
    for dx, dy in greeted:
        pl.semaphore_signal(
            barrier, inc=1, device_id=at(dx, dy), device_id_type=pl.DeviceIdType.MESH
        )
    for copy in loads:
        copy.wait()
    for v in range(8):
        own_strip[v] = strips([own[v, z] for z in range(CZ)])
    pl.semaphore_wait(barrier, len(greeted))

    low, high = pl.ds(0, 4), pl.ds(4, 4)
    plan = [
        (own.at[:, :, high, :], halo.at[:, :, high, :]),
        (own.at[:, :, low, :], halo.at[:, :, low, :]),
        (own_strip, y_strip.at[0]),
        (own_strip, y_strip.at[1]),
        (own_strip.at[:, high, :], d_strip.at[0, :, high, :]),
        (own_strip.at[:, high, :], d_strip.at[1, :, high, :]),
        (own_strip.at[:, low, :], d_strip.at[0, :, low, :]),
        (own_strip.at[:, low, :], d_strip.at[1, :, low, :]),
    ]
    sends = [
        pltpu.make_async_remote_copy(
            src_ref=src, dst_ref=dst, send_sem=send_sem.at[i], recv_sem=recv_sem.at[i],
            device_id=at(*HALOS[i]), device_id_type=pl.DeviceIdType.MESH,
        )
        for i, (src, dst) in enumerate(plan)
    ]
    for copy in sends:
        copy.start()
    for copy in sends:
        copy.wait_recv()

    lane = lanes() % 32
    for v in range(8):
        for z in range(CZ):
            state[v, z, 0:8] = own[v, z]
            state[v, z, 8:16] = halo[v, z]
        state[v, EDGE, 0:8] = jnp.where(
            lane < 8, y_strip[0, v], jnp.where(lane < 24, own_strip[v], y_strip[1, v])
        )
        state[v, EDGE, 8:16] = jnp.where(
            lane < 8,
            d_strip[0, v],
            jnp.where(lane < 24, strips([halo[v, z] for z in range(CZ)]), d_strip[1, v]),
        )
    for k in range(CHUNKS):
        for c in range(3):
            cell[c, k] = 0.5 * (state[5 + c, k] + shifted(state, 5 + c, k, -1, c))

    best = None
    for z in range(CZ):
        rho, pres = state[0, z, 0:8], state[4, z, 0:8]
        sq = [cell[c, z, 0:8] * cell[c, z, 0:8] for c in range(3)]
        for c in range(3):
            value = jnp.abs(state[1 + c, z, 0:8]) + fast(
                rho, pres, sq[c], sq[(c + 1) % 3] + sq[(c + 2) % 3]
            )
            best = value if best is None else jnp.maximum(best, value)
    top = jnp.max(best, axis=0, keepdims=True)

    first_slot = [sum(len(s) for s in stages[:i]) for i in range(len(stages))]
    started = []

    def stage_start(i, value):
        top_send[i] = value
        copies = []
        for j, (dx, dy) in enumerate(stages[i]):
            slot = first_slot[i] + j
            copy = pltpu.make_async_remote_copy(
                src_ref=top_send.at[i], dst_ref=top_recv.at[slot],
                send_sem=tsend_sem.at[slot], recv_sem=trecv_sem.at[slot],
                device_id=at(dx, dy), device_id_type=pl.DeviceIdType.MESH,
            )
            copy.start()
            copies.append(copy)
        started.append(copies)

    def stage_end(i, value):
        for copy in started[i]:
            copy.wait_recv()
        for j in range(len(stages[i])):
            value = jnp.maximum(value, top_recv[first_slot[i] + j])
        return value

    stage_start(0, top)
    for c in range(3):
        one, two = (c + 1) % 3, (c + 2) % 3
        for k in range(CHUNKS):
            names = [(state, 0), (state, 1 + c), (state, 1 + one), (state, 1 + two), (state, 4),
                     (cell, one), (cell, two)]
            left = [shifted(ref, v, k, 1, c) for ref, v in names]
            right = [ref[v, k] for ref, v in names]
            put_flux(flux, c, k, hlle(left, right, state[5 + c, k]))
        if c + 1 < min(3, len(stages)):
            top = stage_end(c, top)
            stage_start(c + 1, top)
    edges(flux, edge, range(CHUNKS))
    for k in range(CHUNKS):
        for v in range(5):
            change[v, k] = div_part(flux, v, k)
        for c in range(3):
            change[5 + c, k] = curl_parts(edge, c, k)
    for i in range(min(3, len(stages)) - 1, len(stages)):
        top = stage_end(i, top)
        if i + 1 < len(stages):
            stage_start(i + 1, top)
    step = CFL / jnp.broadcast_to(jnp.max(top, axis=1, keepdims=True), (1, CY))
    step_out[0] = jnp.max(step)
    semi = 0.5 * step

    for k in range(CHUNKS):
        for c in range(3):
            half[5 + c, k] = state[5 + c, k] - semi * change[5 + c, k]
    for k in range(CHUNKS):
        rho, pres = state[0, k], state[4, k]
        vel = [state[1 + c, k] for c in range(3)]
        mag = [cell[c, k] for c in range(3)]
        energy = (
            1.5 * pres
            + (0.5 * rho) * (vel[0] * vel[0] + vel[1] * vel[1] + vel[2] * vel[2])
            + 0.5 * (mag[0] * mag[0] + mag[1] * mag[1] + mag[2] * mag[2])
        )
        if k < EDGE:
            result[0, k] = energy[0:8]
        hrho = rho - semi * change[0, k]
        inv = 1.0 / hrho
        mom = [rho * vel[c] - semi * change[1 + c, k] for c in range(3)]
        energy = energy - semi * change[4, k]
        hmag = [0.5 * (half[5 + c, k] + shifted(half, 5 + c, k, -1, c)) for c in range(3)]
        msq = mom[0] * mom[0] + mom[1] * mom[1] + mom[2] * mom[2]
        bsq = hmag[0] * hmag[0] + hmag[1] * hmag[1] + hmag[2] * hmag[2]
        half[0, k] = hrho
        for c in range(3):
            half[1 + c, k] = mom[c] * inv
            hcell[c, k] = hmag[c]
        half[4, k] = (GAMMA - 1.0) * (energy - 0.5 * (msq * inv) - 0.5 * bsq)

    for c in range(3):
        one, two = (c + 1) % 3, (c + 2) % 3
        names = [(half, 0), (half, 1 + c), (half, 1 + one), (half, 1 + two), (half, 4),
                 (hcell, one), (hcell, two)]
        for k in range(CHUNKS):
            for i, (ref, v) in enumerate(names):
                q = ref[v, k]
                a = q - shifted(ref, v, k, 1, c)
                b = shifted(ref, v, k, -1, c) - q
                g = 0.5 * (
                    jnp.maximum(jnp.minimum(a, b), 0.0) + jnp.minimum(jnp.maximum(a, b), 0.0)
                )
                lefts[7 * c + i, k] = q + g
                rights[7 * c + i, k] = q - g
        for k in range(CHUNKS):
            left = [shifted(lefts, 7 * c + i, k, 1, c) for i in range(7)]
            right = [rights[7 * c + i, k] for i in range(7)]
            put_flux(flux, c, k, hlle(left, right, half[5 + c, k]))
    edges(flux, edge, range(CHUNKS))
    for z in range(CZ):
        rho = state[0, z, 0:8]
        for v in range(5):
            start = rho if v == 0 else result[0, z] if v == 4 else rho * state[v, z, 0:8]
            value = start - step * div_part(flux, v, z)[0:8]
            if v == 0:
                rho_out[z] = value
            elif v == 4:
                ener_out[z] = value
            else:
                mom_out[v - 1, z] = value
        for c in range(3):
            face_out[c, z] = state[5 + c, z, 0:8] - step * curl_parts(edge, c, z)[0:8]

    for copy in sends:
        copy.wait_send()
    for copies in started:
        for copy in copies:
            copy.wait_send()


def on_device(nbx, nby, density, velocity, pressure, field):
    stages = max_stages(nbx, nby)
    slots = sum(len(s) for s in stages)
    f32 = jnp.float32
    wide = (CHUNKS, 2 * CX, CY)
    out = pl.pallas_call(
        functools.partial(kernel, nbx, nby, stages),
        out_shape=[
            jax.ShapeDtypeStruct((CZ, CX, CY), f32),
            jax.ShapeDtypeStruct((3, CZ, CX, CY), f32),
            jax.ShapeDtypeStruct((CZ, CX, CY), f32),
            jax.ShapeDtypeStruct((3, CZ, CX, CY), f32),
            jax.ShapeDtypeStruct((1,), f32),
        ],
        in_specs=[pl.BlockSpec(memory_space=pl.ANY)] * 4,
        out_specs=[pl.BlockSpec(memory_space=pltpu.VMEM)] * 4
        + [pl.BlockSpec(memory_space=pltpu.SMEM)],
        scratch_shapes=[
            pltpu.VMEM((8, CZ, CX, CY), f32),
            pltpu.VMEM((8, CX, CY), f32),
            pltpu.VMEM((8, CZ, CX, CY), f32),
            pltpu.VMEM((2, 8, CX, CY), f32),
            pltpu.VMEM((2, 8, CX, CY), f32),
            pltpu.VMEM((len(stages), 1, CY), f32),
            pltpu.VMEM((slots, 1, CY), f32),
            pltpu.VMEM((8,) + wide, f32),
            pltpu.VMEM((3,) + wide, f32),
            pltpu.VMEM((21,) + wide, f32),
            pltpu.VMEM((3,) + wide, f32),
            pltpu.VMEM((8,) + wide, f32),
            pltpu.VMEM((8,) + wide, f32),
            pltpu.VMEM((3,) + wide, f32),
            pltpu.VMEM((21,) + wide, f32),
            pltpu.VMEM((21,) + wide, f32),
            pltpu.VMEM((1, CZ, CX, CY), f32),
            pltpu.SemaphoreType.DMA((4,)),
            pltpu.SemaphoreType.DMA((4,)),
            pltpu.SemaphoreType.DMA((8,)),
            pltpu.SemaphoreType.DMA((8,)),
            pltpu.SemaphoreType.DMA((slots,)),
            pltpu.SemaphoreType.DMA((slots,)),
        ],
        compiler_params=pltpu.CompilerParams(
            collective_id=0, has_side_effects=True, vmem_limit_bytes=32 * 1024 * 1024
        ),
    )(density, velocity, pressure, field)
    return (out[0], out[1], out[2], out[3], out[4].reshape(()))


def solution(mesh):
    in_specs = (
        P(None, "bx", "by"),
        P(None, None, "bx", "by"),
        P(None, "bx", "by"),
        P(None, None, "bx", "by"),
    )
    out_specs = in_specs + (P(),)
    return jax.shard_map(
        functools.partial(on_device, mesh.shape["bx"], mesh.shape["by"]),
        mesh=mesh, in_specs=in_specs, out_specs=out_specs, check_vma=False,
    )
```

time: 132 us -> 29.9 us (0.23)
  blocking collectives: 40.4 us -> 0 us
  local copies, waits for them, and re-layouts: 44.6 us -> 5.47 us
  Pallas kernels: 0 us -> 21.6 us
  other arithmetic: 21 us -> 0 us
  starting transfers between devices: 13.9 us -> 0 us
  waiting for transfers between devices: 6.84 us -> 0 us
  between operations: 4.36 us -> 2.4 us
    pmax x1 -> x0, blocking collectives: 40.4 us -> none  [on_device(): top = lax.pmax(jnp.max(trimmed(speeds(wide), first_rim)), ('bx', 'by'))]
    concatenate x220 -> x0, local copies, waits for them, and re-layouts: 36 us -> none  [moved(): return jnp.roll(array, by, AXES[comp])]
    pallas_call x0 -> x1, Pallas kernels: none -> 21.6 us  [on_device(): pl.pallas_call(functools.partial(kernel, nbx, nby, stages), out_shape=[ja...]
    ppermute x8 -> x0, starting transfers between devices: 13.9 us -> none  [the longest x4 8.4 us: with_halo(): lax.ppermute(head, axis, [((i + 1) % count, i) for i in range(count)])]
    unnamed x17 -> x0, other arithmetic: 8.21 us -> none
    ppermute x8 -> x0, waiting for transfers between devices: 6.84 us -> none  [the longest x4 6.08 us: with_halo(): lax.ppermute(tail, axis, [(i, (i + 1) % count) for i in range(count)])]
    div x34 -> x0, other arithmetic: 6.55 us -> none  [hlle(): (upper * flux_left[v] - lower * flux_right[v] + lower * upper * (cons_rig...]
    slice x14 -> x0, local copies, waits for them, and re-layouts: 3.21 us -> none  [the longest x8 2.05 us: moved(): return jnp.roll(array, by, AXES[comp])]
  transfers between devices with their start and end apart: 8 -> 0, of which waited for: 6 -> 0; matrix products, arithmetic and copies ran while one was open for 0% -> 0% of each run, Pallas kernels for 0% -> 0%
where the time goes in v1:
time: 29.9 us; the launch traced here: 29.5 us
  Pallas kernels  21.6 us (72%)
  local copies, waits for them, and re-layouts  5.47 us (18%)
  between operations  2.4 us (8%)
    pallas_call x1, Pallas kernels, on_device(): pl.pallas_call(functools.partial(kernel, nbx, nby, stages), out_shape=[ja...  21.6 us
    unnamed x12, local copies, waits for them, and re-layouts  5.47 us

profile of v1, /device:TPU:0, one launch (start us, length us, event | category | flops | bytes accessed | tf_op | source)
XLA Modules:
  0.0 29.5 jit_solution(11131818411393590985)
XLA Ops:
  0.6 0.0 copy-start
  0.6 0.8 %copy-done = f32[3,4,8,128]{3,2,1,0:T(8,128)S(1)} copy-done((f32[3,4,8,128]{3,2,1,0:T(8,128)S(1)}, f32[3,4,8,128]{3,2,1,0:T(8,128)}, u32[]{:S(2)}) %copy-start) | copy-done | bytes 49176
  1.4 0.0 copy-start.1
  1.4 0.8 %copy-done.1 = f32[3,4,8,128]{3,2,1,0:T(8,128)S(1)} copy-done((f32[3,4,8,128]{3,2,1,0:T(8,128)S(1)}, f32[3,4,8,128]{3,2,1,0:T(8,128)}, u32[]{:S(2)}) %copy-start.1) | copy-done | bytes 49176
  2.2 0.0 copy-start.2
  2.2 0.7 %copy-done.2 = f32[4,8,128]{2,1,0:T(8,128)S(1)} copy-done((f32[4,8,128]{2,1,0:T(8,128)S(1)}, f32[4,8,128]{2,1,0:T(8,128)}, u32[]{:S(2)}) %copy-start.2) | copy-done | bytes 16408
  2.9 0.0 copy-start.3
  3.0 0.7 %copy-done.3 = f32[4,8,128]{2,1,0:T(8,128)S(1)} copy-done((f32[4,8,128]{2,1,0:T(8,128)S(1)}, f32[4,8,128]{2,1,0:T(8,128)}, u32[]{:S(2)}) %copy-start.3) | copy-done | bytes 16408
  3.7 21.6 %shard_map.83 = (f32[4,8,128]{2,1,0:T(8,128)S(1)}, f32[3,4,8,128]{3,2,1,0:T(8,128)S(1)}, f32[4,8,128]{2,1,0:T(8,128)S(1)}, f32[3,4,8,128]{3,2,1,0:T(8,128)S(1)}, f32[1]{0:T(128)}) custom-call(f32[4,8,128]{2,1,0:T(8,128)S(1)} %copy-done.2, f32[3,4,8,128]{3,2,1,0:T(8,128)S(1)} %copy-done, f32[4,8,128]{2,1,0:T(8,128)S(1)} %copy-done.3, ...), custom_call_target="tpu_custom_call" | custom-call | tf_op jit(solution)/shard_map/pallas_call | solution.py:349
  25.3 0.6 %copy.14 = f32[4,8,128]{2,1,0:T(8,128)} copy(f32[4,8,128]{2,1,0:T(8,128)S(1)} %get-tuple-element.20) | data formatting | bytes 32768
  25.9 0.6 %copy.15 = f32[3,4,8,128]{3,2,1,0:T(8,128)} copy(f32[3,4,8,128]{3,2,1,0:T(8,128)S(1)} %get-tuple-element.21) | data formatting | bytes 98304
  26.5 0.6 %copy.16 = f32[4,8,128]{2,1,0:T(8,128)} copy(f32[4,8,128]{2,1,0:T(8,128)S(1)} %get-tuple-element.22) | data formatting | bytes 32768
  27.1 0.6 %copy.17 = f32[3,4,8,128]{3,2,1,0:T(8,128)} copy(f32[3,4,8,128]{3,2,1,0:T(8,128)S(1)} %get-tuple-element.23) | data formatting | bytes 98304
Async XLA Ops:
  0.6 0.8 %copy-start = (f32[3,4,8,128]{3,2,1,0:T(8,128)S(1)}, f32[3,4,8,128]{3,2,1,0:T(8,128)}, u32[]{:S(2)}) copy-start(f32[3,4,8,128]{3,2,1,0:T(8,128)} %vel_in.1) | copy-start | bytes 147460
  1.4 0.8 %copy-start.1 = (f32[3,4,8,128]{3,2,1,0:T(8,128)S(1)}, f32[3,4,8,128]{3,2,1,0:T(8,128)}, u32[]{:S(2)}) copy-start(f32[3,4,8,128]{3,2,1,0:T(8,128)} %face_in.1) | copy-start | bytes 147460
  2.2 0.7 %copy-start.2 = (f32[4,8,128]{2,1,0:T(8,128)S(1)}, f32[4,8,128]{2,1,0:T(8,128)}, u32[]{:S(2)}) copy-start(f32[4,8,128]{2,1,0:T(8,128)} %rho_in.1) | copy-start | bytes 49156
  2.9 0.7 %copy-start.3 = (f32[4,8,128]{2,1,0:T(8,128)S(1)}, f32[4,8,128]{2,1,0:T(8,128)}, u32[]{:S(2)}) copy-start(f32[4,8,128]{2,1,0:T(8,128)} %pres_in.1) | copy-start | bytes 49156

commit v2 on v1

--- a/solution.py
+++ b/solution.py
@@ -13,10 +13,12 @@
 CZ, CX, CY = 4, 8, 128
 EDGE = 4
 CHUNKS = 5
-HALOS = ((1, 0), (-1, 0), (0, 1), (0, -1), (1, 1), (1, -1), (-1, 1), (-1, -1))
+HALOS = ((-1, 0), (0, -1), (1, 0), (-1, 0), (1, 1), (-1, 1), (0, 1), (1, -1), (-1, -1), (0, -1))
 
 
 def max_stages(nbx, nby):
+    if nbx * nby <= 32:
+        return [[(x, y) for x in range(nbx) for y in range(nby) if (x, y) != (0, 0)]]
     stages = [[(0, o) for o in range(1, nby)]]
     window = 1
     while window < nbx:
@@ -140,7 +142,7 @@
     nbx, nby, stages,
     rho_in, vel_in, pres_in, face_in,
     rho_out, mom_out, ener_out, face_out, step_out,
-    own, own_strip, halo, y_strip, d_strip, top_send, top_recv,
+    own, own_strip, x_edge, y_edge, halo, y_strip, d_strip, top_send, top_recv,
     state, cell, flux, edge, change, half, hcell, lefts, rights, result,
     in_sem, out_sem, send_sem, recv_sem, tsend_sem, trecv_sem,
 ):
@@ -174,16 +176,21 @@
     pl.semaphore_wait(barrier, len(greeted))
 
     low, high = pl.ds(0, 4), pl.ds(4, 4)
+    other = 0 if nby == 2 else 1
     plan = [
+        (own.at[5, :, pl.ds(0, 1), :], x_edge.at[:, pl.ds(0, 1), :]),
+        (own_strip.at[6], y_edge),
         (own.at[:, :, high, :], halo.at[:, :, high, :]),
         (own.at[:, :, low, :], halo.at[:, :, low, :]),
+        (own_strip.at[:, high, :], d_strip.at[0, :, high, :]),
+        (own_strip.at[:, low, :], d_strip.at[0, :, low, :]),
         (own_strip, y_strip.at[0]),
-        (own_strip, y_strip.at[1]),
-        (own_strip.at[:, high, :], d_strip.at[0, :, high, :]),
-        (own_strip.at[:, high, :], d_strip.at[1, :, high, :]),
-        (own_strip.at[:, low, :], d_strip.at[0, :, low, :]),
-        (own_strip.at[:, low, :], d_strip.at[1, :, low, :]),
+        (own_strip.at[:, high, :], d_strip.at[other, :, high, :]),
+        (own_strip.at[:, low, :], d_strip.at[other, :, low, :]),
+        (own_strip, y_strip.at[other]),
     ]
+    if nby == 2:
+        plan = plan[:7]
     sends = [
         pltpu.make_async_remote_copy(
             src_ref=src, dst_ref=dst, send_sem=send_sem.at[i], recv_sem=recv_sem.at[i],
@@ -193,34 +200,24 @@
     ]
     for copy in sends:
         copy.start()
-    for copy in sends:
+    for copy in sends[:2]:
         copy.wait_recv()
 
-    lane = lanes() % 32
-    for v in range(8):
-        for z in range(CZ):
-            state[v, z, 0:8] = own[v, z]
-            state[v, z, 8:16] = halo[v, z]
-        state[v, EDGE, 0:8] = jnp.where(
-            lane < 8, y_strip[0, v], jnp.where(lane < 24, own_strip[v], y_strip[1, v])
-        )
-        state[v, EDGE, 8:16] = jnp.where(
-            lane < 8,
-            d_strip[0, v],
-            jnp.where(lane < 24, strips([halo[v, z] for z in range(CZ)]), d_strip[1, v]),
-        )
-    for k in range(CHUNKS):
-        for c in range(3):
-            cell[c, k] = 0.5 * (state[5 + c, k] + shifted(state, 5 + c, k, -1, c))
-
     best = None
+    last_row = lax.broadcasted_iota(jnp.int32, (CX, 1), 0) == CX - 1
+    last_lane = lanes() == CY - 1
     for z in range(CZ):
-        rho, pres = state[0, z, 0:8], state[4, z, 0:8]
-        sq = [cell[c, z, 0:8] * cell[c, z, 0:8] for c in range(3)]
-        for c in range(3):
-            value = jnp.abs(state[1 + c, z, 0:8]) + fast(
-                rho, pres, sq[c], sq[(c + 1) % 3] + sq[(c + 2) % 3]
-            )
+        rho, pres = own[0, z], own[4, z]
+        face = [own[5 + c, z] for c in range(3)]
+        after = [
+            jnp.where(last_row, x_edge[z, 0:1], roll(face[0], -1, 0)),
+            jnp.where(last_lane, roll(y_edge[...], CY - 1 - (32 * z + 24), 1), roll(face[1], -1, 1)),
+            own[7, (z + 1) % CZ],
+        ]
+        mag = [0.5 * (face[c] + after[c]) for c in range(3)]
+        sq = [m * m for m in mag]
+        for c in range(3):
+            value = jnp.abs(own[1 + c, z]) + fast(rho, pres, sq[c], sq[(c + 1) % 3] + sq[(c + 2) % 3])
             best = value if best is None else jnp.maximum(best, value)
     top = jnp.max(best, axis=0, keepdims=True)
 
@@ -249,6 +246,26 @@
         return value
 
     stage_start(0, top)
+    for copy in sends[2:]:
+        copy.wait_recv()
+
+    lane = lanes() % 32
+    for v in range(8):
+        for z in range(CZ):
+            state[v, z, 0:8] = own[v, z]
+            state[v, z, 8:16] = halo[v, z]
+        state[v, EDGE, 0:8] = jnp.where(
+            lane < 8, y_strip[0, v], jnp.where(lane < 24, own_strip[v], y_strip[other, v])
+        )
+        state[v, EDGE, 8:16] = jnp.where(
+            lane < 8,
+            d_strip[0, v],
+            jnp.where(lane < 24, strips([halo[v, z] for z in range(CZ)]), d_strip[other, v]),
+        )
+    for k in range(CHUNKS):
+        for c in range(3):
+            cell[c, k] = 0.5 * (state[5 + c, k] + shifted(state, 5 + c, k, -1, c))
+
     for c in range(3):
         one, two = (c + 1) % 3, (c + 2) % 3
         for k in range(CHUNKS):
@@ -341,9 +358,19 @@
             copy.wait_send()
 
 
+def hand_on(*refs):
+    sem = refs[8]
+    copies = [pltpu.make_async_copy(refs[i], refs[4 + i], sem.at[i]) for i in range(4)]
+    for copy in copies:
+        copy.start()
+    for copy in copies:
+        copy.wait()
+
+
 def on_device(nbx, nby, density, velocity, pressure, field):
     stages = max_stages(nbx, nby)
     slots = sum(len(s) for s in stages)
+    sides = 1 if nby == 2 else 2
     f32 = jnp.float32
     wide = (CHUNKS, 2 * CX, CY)
     out = pl.pallas_call(
@@ -361,9 +388,11 @@
         scratch_shapes=[
             pltpu.VMEM((8, CZ, CX, CY), f32),
             pltpu.VMEM((8, CX, CY), f32),
+            pltpu.VMEM((CZ, CX, CY), f32),
+            pltpu.VMEM((CX, CY), f32),
             pltpu.VMEM((8, CZ, CX, CY), f32),
-            pltpu.VMEM((2, 8, CX, CY), f32),
-            pltpu.VMEM((2, 8, CX, CY), f32),
+            pltpu.VMEM((sides, 8, CX, CY), f32),
+            pltpu.VMEM((sides, 8, CX, CY), f32),
             pltpu.VMEM((len(stages), 1, CY), f32),
             pltpu.VMEM((slots, 1, CY), f32),
             pltpu.VMEM((8,) + wide, f32),
@@ -378,16 +407,23 @@
             pltpu.VMEM((1, CZ, CX, CY), f32),
             pltpu.SemaphoreType.DMA((4,)),
             pltpu.SemaphoreType.DMA((4,)),
-            pltpu.SemaphoreType.DMA((8,)),
-            pltpu.SemaphoreType.DMA((8,)),
+            pltpu.SemaphoreType.DMA((len(HALOS),)),
+            pltpu.SemaphoreType.DMA((len(HALOS),)),
             pltpu.SemaphoreType.DMA((slots,)),
             pltpu.SemaphoreType.DMA((slots,)),
         ],
         compiler_params=pltpu.CompilerParams(
-            collective_id=0, has_side_effects=True, vmem_limit_bytes=32 * 1024 * 1024
+            collective_id=0, has_side_effects=True, vmem_limit_bytes=60 * 1024 * 1024
         ),
     )(density, velocity, pressure, field)
-    return (out[0], out[1], out[2], out[3], out[4].reshape(()))
+    final = pl.pallas_call(
+        hand_on,
+        out_shape=[jax.ShapeDtypeStruct(a.shape, f32) for a in out[:4]],
+        in_specs=[pl.BlockSpec(memory_space=pltpu.VMEM)] * 4,
+        out_specs=[pl.BlockSpec(memory_space=pl.ANY)] * 4,
+        scratch_shapes=[pltpu.SemaphoreType.DMA((4,))],
+    )(*out[:4])
+    return (*final, out[4].reshape(()))
 
 
 def solution(mesh):

time: 29.9 us -> 22.7 us (0.76)
  local copies, waits for them, and re-layouts: 5.47 us -> 0 us
  Pallas kernels: 21.6 us -> 20.1 us
    unnamed x12 -> x0, local copies, waits for them, and re-layouts: 5.47 us -> none
    pallas_call x1, Pallas kernels: 21.6 us -> 18.5 us  [on_device(): pl.pallas_call(functools.partial(kernel, nbx, nby, stages), out_shape=[ja...]
    pallas_call x0 -> x1, Pallas kernels: none -> 1.54 us  [on_device(): pl.pallas_call(hand_on, out_shape=[jax.ShapeDtypeStruct(a.shape, f32) for...]
where the time goes in v2:
time: 22.7 us; the launch traced here: 22.5 us
  Pallas kernels  20.1 us (89%)
  between operations  2.4 us (11%)
    pallas_call x1, Pallas kernels, on_device(): pl.pallas_call(functools.partial(kernel, nbx, nby, stages), out_shape=[ja...  18.5 us
    pallas_call x1, Pallas kernels, on_device(): pl.pallas_call(hand_on, out_shape=[jax.ShapeDtypeStruct(a.shape, f32) for...  1.54 us

profile of v2, /device:TPU:0, one launch (start us, length us, event | category | flops | bytes accessed | tf_op | source)
XLA Modules:
  0.0 22.5 jit_solution(15932616759435032731)
XLA Ops:
  0.6 18.5 %shard_map.83 = (f32[4,8,128]{2,1,0:T(8,128)}, f32[3,4,8,128]{3,2,1,0:T(8,128)}, f32[4,8,128]{2,1,0:T(8,128)}, f32[3,4,8,128]{3,2,1,0:T(8,128)}, f32[1]{0:T(128)}) custom-call(f32[4,8,128]{2,1,0:T(8,128)} %rho_in.1, f32[3,4,8,128]{3,2,1,0:T(8,128)} %vel_in.1, f32[4,8,128]{2,1,0:T(8,128)} %pres_in.1, f32[3,4,8,128]{3,2,1,0:T(8,128)} %face_in.1), custom_call_target="tpu_custom_call" | custom-call | tf_op jit(solution)/shard_map/pallas_call | solution.py:376
  19.2 1.5 %shard_map.84 = (f32[4,8,128]{2,1,0:T(8,128)}, f32[3,4,8,128]{3,2,1,0:T(8,128)}, f32[4,8,128]{2,1,0:T(8,128)}, f32[3,4,8,128]{3,2,1,0:T(8,128)}) custom-call(f32[4,8,128]{2,1,0:T(8,128)} %get-tuple-element.14.refs_0_, f32[3,4,8,128]{3,2,1,0:T(8,128)} %get-tuple-element.15.refs_1_, f32[4,8,128]{2,1,0:T(8,128)} %get-tuple-element.16.refs_2_, ...), custom_call_target="tpu_custom_call" | custom-call | tf_op jit(solution)/shard_map/pallas_call | solution.py:419

commit v3 on v2

--- a/solution.py
+++ b/solution.py
@@ -18,7 +18,7 @@
 
 def max_stages(nbx, nby):
     if nbx * nby <= 32:
-        return [[(x, y) for x in range(nbx) for y in range(nby) if (x, y) != (0, 0)]]
+        return [[(0, y) for y in range(1, nby)], [(x, 0) for x in range(1, nbx)]]
     stages = [[(0, o) for o in range(1, nby)]]
     window = 1
     while window < nbx:
@@ -139,7 +139,7 @@
 
 
 def kernel(
-    nbx, nby, stages,
+    nbx, nby, stages, early,
     rho_in, vel_in, pres_in, face_in,
     rho_out, mom_out, ener_out, face_out, step_out,
     own, own_strip, x_edge, y_edge, halo, y_strip, d_strip, top_send, top_recv,
@@ -246,6 +246,9 @@
         return value
 
     stage_start(0, top)
+    for i in range(early):
+        top = stage_end(i, top)
+        stage_start(i + 1, top)
     for copy in sends[2:]:
         copy.wait_recv()
 
@@ -274,16 +277,13 @@
             left = [shifted(ref, v, k, 1, c) for ref, v in names]
             right = [ref[v, k] for ref, v in names]
             put_flux(flux, c, k, hlle(left, right, state[5 + c, k]))
-        if c + 1 < min(3, len(stages)):
-            top = stage_end(c, top)
-            stage_start(c + 1, top)
     edges(flux, edge, range(CHUNKS))
     for k in range(CHUNKS):
         for v in range(5):
             change[v, k] = div_part(flux, v, k)
         for c in range(3):
             change[5 + c, k] = curl_parts(edge, c, k)
-    for i in range(min(3, len(stages)) - 1, len(stages)):
+    for i in range(early, len(stages)):
         top = stage_end(i, top)
         if i + 1 < len(stages):
             stage_start(i + 1, top)
@@ -374,7 +374,7 @@
     f32 = jnp.float32
     wide = (CHUNKS, 2 * CX, CY)
     out = pl.pallas_call(
-        functools.partial(kernel, nbx, nby, stages),
+        functools.partial(kernel, nbx, nby, stages, len(stages) - 1),
         out_shape=[
             jax.ShapeDtypeStruct((CZ, CX, CY), f32),
             jax.ShapeDtypeStruct((3, CZ, CX, CY), f32),

time: 22.7 us -> 22.4 us (0.987)
  Pallas kernels: 20.1 us -> 19.7 us
    pallas_call x1, Pallas kernels: 18.5 us -> 18.2 us  [on_device(): pl.pallas_call(functools.partial(kernel, nbx, nby, stages, len(stages) -...]
where the time goes in v3:
time: 22.4 us; the launch traced here: 22.1 us
  Pallas kernels  19.7 us (88%)
  between operations  2.4 us (11%)
    pallas_call x1, Pallas kernels, on_device(): pl.pallas_call(functools.partial(kernel, nbx, nby, stages, len(stages) -...  18.2 us
    pallas_call x1, Pallas kernels, on_device(): pl.pallas_call(hand_on, out_shape=[jax.ShapeDtypeStruct(a.shape, f32) for...  1.54 us

profile of v3, /device:TPU:0, one launch (start us, length us, event | category | flops | bytes accessed | tf_op | source)
XLA Modules:
  0.0 22.1 jit_solution(16171093236639103906)
XLA Ops:
  0.6 18.2 %shard_map.83 = (f32[4,8,128]{2,1,0:T(8,128)}, f32[3,4,8,128]{3,2,1,0:T(8,128)}, f32[4,8,128]{2,1,0:T(8,128)}, f32[3,4,8,128]{3,2,1,0:T(8,128)}, f32[1]{0:T(128)}) custom-call(f32[4,8,128]{2,1,0:T(8,128)} %rho_in.1, f32[3,4,8,128]{3,2,1,0:T(8,128)} %vel_in.1, f32[4,8,128]{2,1,0:T(8,128)} %pres_in.1, f32[3,4,8,128]{3,2,1,0:T(8,128)} %face_in.1), custom_call_target="tpu_custom_call" | custom-call | tf_op jit(solution)/shard_map/pallas_call | solution.py:376
  18.8 1.5 %shard_map.84 = (f32[4,8,128]{2,1,0:T(8,128)}, f32[3,4,8,128]{3,2,1,0:T(8,128)}, f32[4,8,128]{2,1,0:T(8,128)}, f32[3,4,8,128]{3,2,1,0:T(8,128)}) custom-call(f32[4,8,128]{2,1,0:T(8,128)} %get-tuple-element.14.refs_0_, f32[3,4,8,128]{3,2,1,0:T(8,128)} %get-tuple-element.15.refs_1_, f32[4,8,128]{2,1,0:T(8,128)} %get-tuple-element.16.refs_2_, ...), custom_call_target="tpu_custom_call" | custom-call | tf_op jit(solution)/shard_map/pallas_call | solution.py:419
